TPU v7x, 128 devices: a whole 4x4x4 slice. The times are simulated.
128 devices in a mesh: rows: 32 (over z_hi, x, y), feat: 4 (over z_lo, core).
Axes of the slice: x: 4, y: 4, z: 4 (z_hi: 2, z_lo: 2; z = z_hi * 2 + z_lo), core: 2. Of those that a mesh axis runs over, the one named last changes fastest.
Arguments:
- features: bfloat16 [256, 196608], P('feat', 'rows'), may hold values from -6 to 6
- weight: bfloat16 [256, 256], P('feat'), may hold values from -0.375 to 0.375
- cotangent: bfloat16 [256, 196608], P('feat', 'rows'), may hold values from -6 to 6
- blocks: bfloat16 [32, 256, 128, 128], P('rows', 'feat'), may hold values from -0.25 to 0.25
- row_block: int32 [32, 256], P('rows', 'feat'), may hold values from 0 to 47
- src_owner: int32 [32, 256, 1], P('rows', 'feat'), may hold values from 0 to 31; in each aligned block of 64 rows (0 to 63, 64 to 127, ..., all dimensions but the last counted through in order) at most 4 rows name the same one
- src_block: int32 [32, 256], P('rows', 'feat'), may hold values from 0 to 47
- live: int32 [32, 4], P('rows', 'feat'), may hold values from 8 to 64, as said below
Outputs:
- activation: bfloat16 [256, 196608], P('feat', 'rows')
- feature_grad: bfloat16 [256, 196608], P('feat', 'rows')
- weight_grad: float32 [256, 256], P('feat')
Inputs may be any that keep to these rules, and one draw needn't show every extreme that they name: `src_owner`: among the 64 slots of one device, no owner is named more than 4 times, a bound that some block reaches. Some device has all 64 slots live.
All inputs are finite; a program needn't handle non-finite values.
Results may differ from a plain program's by a relative error of at most 0.024.
Values may be sent and summed in bfloat16 or wider, within the bound.
No kernel may reach another device: no remote copies, remote signals or barrier semaphores. Data moves between devices by JAX's collectives and lax.ppermute only.
A program may use at most 128 MiB of HBM per device.

v0:
```python
import functools
import math

import jax
import jax.numpy as jnp
from jax import lax
from jax.experimental import pallas as pl
from jax.experimental.pallas import tpu as pltpu
from jax.sharding import PartitionSpec as P

BF = jnp.bfloat16
F32 = jnp.float32
I32 = jnp.int32
VMEM_LIMIT = 56 * 1024 * 1024
GROUP = 8
STRIDE = 16
UNROLL = 7
EDGE = 32
EXTRA = 2
HEAD = 40


def params():
    return pltpu.CompilerParams(vmem_limit_bytes=VMEM_LIMIT)


def core_swap(x):
    return lax.ppermute(x, "feat", [(0, 1), (1, 0), (2, 3), (3, 2)])


def chip_swap(x):
    return lax.ppermute(x, "feat", [(0, 2), (2, 0), (1, 3), (3, 1)])


def gather_feat(x):
    far = chip_swap(x)
    return (x, core_swap(x), far, core_swap(far))


def relative(x, axis, me):
    a = jnp.split(x, 4, axis=axis)
    low = (me & 1) == 1
    high = (me & 2) == 2
    b = [jnp.where(low, a[i ^ 1], a[i]) for i in range(4)]
    c = [jnp.where(high, b[i ^ 2], b[i]) for i in range(4)]
    return jnp.concatenate(c, axis=axis)


def exact_dot(a, b):
    return jnp.dot(a.astype(BF), b.astype(BF), preferred_element_type=F32)


def ranks(want):
    n = want.shape[-1]
    upper = jnp.arange(n)[:, None] < jnp.arange(n)[None, :]
    return exact_dot(want, upper).astype(I32)


def serve_kernel(step, main, index, count, features, out, over):
    width = features.shape[0]
    for i in range(step):
        row = pl.program_id(0) * step + i

        def put(ref, first, k):
            block = jnp.minimum(index[row, k], features.shape[1] // 128 - 1)
            start = pl.multiple_of(block * 128, 128)
            to = pl.multiple_of((k - first) * width, width)
            ref[i, pl.ds(to, width), :] = features[:, pl.ds(start, 128)]

        def body(g, carry):
            for u in range(UNROLL):
                put(out, 0, g * UNROLL + u)
            return carry

        lax.fori_loop(0, (jnp.minimum(count[row], main) + UNROLL - 1) // UNROLL, body, 0)

        @pl.when(count[row] > main)
        def _():
            for k in range(main, main + over.shape[1] // width):
                put(over, main, k)


def serve(features, index, count, rows, main, extra):
    width, nodes = features.shape
    step = 4
    place = lambda r, *_: (r, 0, 0)
    return pl.pallas_call(
        functools.partial(serve_kernel, step, main),
        grid_spec=pltpu.PrefetchScalarGridSpec(
            num_scalar_prefetch=2,
            grid=(rows // step,),
            in_specs=[pl.BlockSpec((width, nodes), lambda r, *_: (0, 0))],
            out_specs=[
                pl.BlockSpec((step, main * width, 128), place),
                pl.BlockSpec((step, extra * width, 128), place),
            ],
        ),
        out_shape=[
            jax.ShapeDtypeStruct((rows, main * width, 128), BF),
            jax.ShapeDtypeStruct((rows, extra * width, 128), BF),
        ],
        compiler_params=params(),
        cost_estimate=pl.CostEstimate(
            flops=0, bytes_accessed=rows * (main + extra) * width * 256, transcendentals=0
        ),
    )(index, count, features)


def tile_copies(lists, tiles, held, sems):
    copies, n = [], 0
    for j in range(lists[0]):
        group = []
        for piece, start, size in lists[1][j]:
            group.append(
                pltpu.make_async_copy(
                    tiles[piece], held.at[j, pl.ds(start, size)], sems.at[n]
                )
            )
            n += 1
        copies.append(group)
    return copies


def aggregate_kernel(lists, slots, place, target, live, flag, panels, over, *refs):
    pieces = sum(len(x) for x in lists[1])
    tiles = refs[:pieces]
    out, held, panel, acc, sems = refs[pieces:]
    blocks = out.shape[0]
    rows, main = panels.shape[:2]
    extra = over.shape[1]
    first = pltpu.make_async_copy(panels, panel.at[pl.ds(0, rows), pl.ds(0, main)], sems.at[pieces])
    first.start()
    copies = tile_copies(lists, tiles, held, sems)
    for group in copies:
        for c in group:
            c.start()
    acc[...] = jnp.zeros_like(acc)

    @pl.when(flag[0] > 0)
    def _():
        more = pltpu.make_async_copy(
            over, panel.at[pl.ds(0, rows), pl.ds(main, extra)], sems.at[pieces + 1]
        )
        more.start()
        more.wait()

    first.wait()
    for j in range(lists[0]):
        for c in copies[j]:
            c.wait()

        def body(g, carry, j=j):
            base = g * GROUP
            products = []
            for u in range(GROUP):
                s = j * slots + base + u
                products.append(
                    lax.dot_general(
                        panel[place[s] >> 6, place[s] & 63],
                        held[j, base + u],
                        (((1,), (1,)), ((), ())),
                        preferred_element_type=F32,
                    )
                )
            for u in range(GROUP):
                t = target[j * slots + base + u]
                acc[t] = acc[t] + products[u]
            return carry

        lax.fori_loop(0, (live[j] + GROUP - 1) // GROUP, body, 0)
    out[...] = acc[:blocks].astype(BF)


def aggregate(panels, over, tiles, lists, slots, place, target, live, flag, blocks):
    size = tiles[0].shape[1]
    rows, main, width, _ = panels.shape
    extra = over.shape[1]
    any_spec = pl.BlockSpec(memory_space=pl.ANY)
    return pl.pallas_call(
        functools.partial(aggregate_kernel, lists, slots),
        grid_spec=pltpu.PrefetchScalarGridSpec(
            num_scalar_prefetch=4,
            grid=(1,),
            in_specs=[any_spec] * (len(tiles) + 2),
            out_specs=pl.BlockSpec((blocks, width, size), lambda i, *_: (0, 0, 0)),
            scratch_shapes=[
                pltpu.VMEM((lists[0], slots, size, size), BF),
                pltpu.VMEM((rows + 1, main + extra, width, size), BF),
                pltpu.VMEM((blocks + 1, width, size), F32),
                pltpu.SemaphoreType.DMA((len(tiles) + 2,)),
            ],
        ),
        out_shape=jax.ShapeDtypeStruct((blocks, width, size), BF),
        compiler_params=params(),
        cost_estimate=pl.CostEstimate(
            flops=2 * lists[0] * slots * width * size * size,
            bytes_accessed=rows * main * width * size * 2 + lists[0] * slots * size * size * 2,
            transcendentals=0,
        ),
    )(place, target, live, flag, panels, over, *tiles)


def middle_kernel(step, weight, a0, a1, a2, a3, c0, c1, c2, c3, act, grad, wgrad, wsum):
    width = a0.shape[1]
    x = jnp.concatenate(
        [jnp.concatenate([a[b] for b in range(step)], axis=1) for a in (a0, a1, a2, a3)], axis=0
    )
    w = weight[...]
    preact = jnp.dot(w, x, preferred_element_type=F32)
    positive = jnp.maximum(preact, 0.0)
    own = positive[:width]
    act[...] = (own * own).astype(BF)
    cot = jnp.concatenate([c[...] for c in (c0, c1, c2, c3)], axis=0)
    pre = (2.0 * cot.astype(F32) * positive).astype(BF)
    g = lax.dot_general(
        w[:, :width], pre, (((0,), (0,)), ((), ())), preferred_element_type=F32
    ).astype(BF)
    for b in range(step):
        grad[b] = g[:, b * 128 : (b + 1) * 128]
    part = lax.dot_general(
        pre[:width], x, (((1,), (1,)), ((), ())), preferred_element_type=F32
    )

    @pl.when(pl.program_id(0) == 0)
    def _():
        wsum[...] = part

    @pl.when(pl.program_id(0) > 0)
    def _():
        wsum[...] = wsum[...] + part

    @pl.when(pl.program_id(0) == pl.num_programs(0) - 1)
    def _():
        for h in range(part.shape[1] // 128):
            wgrad[h * width : (h + 1) * width, :] = wsum[:, h * 128 : (h + 1) * 128].astype(BF)


def middle(weight, aggregated, cotangent):
    blocks, width, size = aggregated[0].shape
    hidden = weight.shape[0]
    step = 8 if blocks % 8 == 0 else 1
    a_spec = pl.BlockSpec((step, width, size), lambda i: (i, 0, 0))
    c_spec = pl.BlockSpec((width, step * size), lambda i: (0, i))
    tall = width * hidden // 128
    w_spec = pl.BlockSpec((tall, 128), lambda i: (0, 0))
    return pl.pallas_call(
        functools.partial(middle_kernel, step),
        grid=(blocks // step,),
        in_specs=[pl.BlockSpec((hidden, hidden), lambda i: (0, 0))] + [a_spec] * 4 + [c_spec] * 4,
        out_specs=[c_spec, a_spec, w_spec],
        out_shape=[
            jax.ShapeDtypeStruct((width, blocks * size), BF),
            jax.ShapeDtypeStruct((blocks, width, size), BF),
            jax.ShapeDtypeStruct((tall, 128), BF),
        ],
        scratch_shapes=[pltpu.VMEM((width, hidden), F32)],
        compiler_params=params(),
        cost_estimate=pl.CostEstimate(
            flops=2 * hidden * (hidden + 2 * width) * blocks * size,
            bytes_accessed=10 * blocks * width * size * 2,
            transcendentals=0,
        ),
    )(weight, *aggregated, *cotangent)


def terms_kernel(lists, slots, place, target, again, live, grads, shares, *refs):
    pieces = sum(len(x) for x in lists[1])
    tiles = refs[:pieces]
    out, over, held, made, sems = refs[pieces:]
    rows, tall = out.shape[:2]
    extra = over.shape[1]
    width = grads.shape[1]
    copies = tile_copies(lists, tiles, held, sems)
    for group in copies:
        for c in group:
            c.start()
    for r in range(rows):
        h = r % (shares.shape[0] // EDGE)
        made[r, :EDGE, :] = shares[h * EDGE : (h + 1) * EDGE, :]
    for j in range(lists[0]):
        for c in copies[j]:
            c.wait()

        def body(g, carry, j=j):
            base = g * GROUP
            products = []
            for u in range(GROUP):
                s = j * slots + base + u
                t = jnp.minimum(target[s], grads.shape[0] - 1)
                products.append(
                    jnp.dot(grads[t], held[j, base + u], preferred_element_type=F32)
                )
            for u in range(GROUP):
                s = j * slots + base + u
                at = pl.ds(pl.multiple_of(EDGE + (place[s] & 63) * width, EDGE), width)
                p = place[s] >> 6
                kept = jnp.where(again[s] > 0, made[p, at, :].astype(F32), 0.0)
                made[p, at, :] = (kept + products[u]).astype(BF)
            return carry

        lax.fori_loop(0, (live[j] + GROUP - 1) // GROUP, body, 0)
    last = [
        pltpu.make_async_copy(made.at[pl.ds(0, rows), pl.ds(0, tall)], out, sems.at[pieces]),
        pltpu.make_async_copy(
            made.at[pl.ds(0, rows), pl.ds(tall, extra)], over, sems.at[pieces + 1]
        ),
    ]
    for c in last:
        c.start()
    for c in last:
        c.wait()


def terms(grads, shares, tiles, lists, slots, place, target, again, live, rows, main, extra):
    size = tiles[0].shape[1]
    blocks, width, _ = grads.shape
    any_spec = pl.BlockSpec(memory_space=pl.ANY)
    return pl.pallas_call(
        functools.partial(terms_kernel, lists, slots),
        grid_spec=pltpu.PrefetchScalarGridSpec(
            num_scalar_prefetch=4,
            grid=(1,),
            in_specs=[
                pl.BlockSpec((blocks, width, size), lambda i, *_: (0, 0, 0)),
                pl.BlockSpec(shares.shape, lambda i, *_: (0, 0)),
            ]
            + [any_spec] * len(tiles),
            out_specs=[any_spec, any_spec],
            scratch_shapes=[
                pltpu.VMEM((lists[0], slots, size, size), BF),
                pltpu.VMEM((rows + 1, EDGE + (main + extra) * width, size), BF),
                pltpu.SemaphoreType.DMA((len(tiles) + 2,)),
            ],
        ),
        out_shape=[
            jax.ShapeDtypeStruct((rows, EDGE + main * width, size), BF),
            jax.ShapeDtypeStruct((rows, extra * width, size), BF),
        ],
        compiler_params=params(),
        cost_estimate=pl.CostEstimate(
            flops=2 * lists[0] * slots * width * size * size,
            bytes_accessed=rows * main * width * size * 2 + lists[0] * slots * size * size * 2,
            transcendentals=0,
        ),
    )(place, target, again, live, grads, shares, *tiles)


def collect_kernel(step, blocks, main, index, count, incoming, over, out, acc):
    width = out.shape[0]

    @pl.when(pl.program_id(0) == 0)
    def _():
        acc[...] = jnp.zeros_like(acc)

    for i in range(step):
        row = pl.program_id(0) * step + i

        def add(ref, shift, k):
            t = index[row, k]
            start = pl.multiple_of(k * width + shift, EDGE)
            acc[t] = acc[t] + ref[i, pl.ds(start, width), :].astype(F32)

        def body(g, carry):
            for u in range(UNROLL):
                add(incoming, EDGE, g * UNROLL + u)
            return carry

        lax.fori_loop(0, (jnp.minimum(count[row], main) + UNROLL - 1) // UNROLL, body, 0)

        @pl.when(count[row] > main)
        def _():
            for k in range(main, main + over.shape[1] // width):
                add(over, -main * width, k)

    @pl.when(pl.program_id(0) == pl.num_programs(0) - 1)
    def _():
        for b in range(blocks):
            out[:, b * 128 : (b + 1) * 128] = acc[b].astype(BF)


def collect(incoming, over, index, count, blocks, width, main, extra):
    rows = incoming.shape[0]
    step = 4
    place = lambda r, *_: (r, 0, 0)
    return pl.pallas_call(
        functools.partial(collect_kernel, step, blocks, main),
        grid_spec=pltpu.PrefetchScalarGridSpec(
            num_scalar_prefetch=2,
            grid=(rows // step,),
            in_specs=[
                pl.BlockSpec((step, EDGE + main * width, 128), place),
                pl.BlockSpec((step, extra * width, 128), place),
            ],
            out_specs=pl.BlockSpec((width, blocks * 128), lambda r, *_: (0, 0)),
            scratch_shapes=[pltpu.VMEM((blocks + 1, width, 128), F32)],
        ),
        out_shape=jax.ShapeDtypeStruct((width, blocks * 128), BF),
        compiler_params=params(),
        cost_estimate=pl.CostEstimate(
            flops=rows * main * width * 128,
            bytes_accessed=rows * main * width * 256,
            transcendentals=0,
        ),
    )(index, count, incoming, over)


def exchange(x):
    return lax.all_to_all(x, "rows", split_axis=0, concat_axis=0, tiled=True)


def exchange_both(main, over, needed):
    over = lax.cond(needed, exchange, lambda x: x, over)
    main, over = lax.optimization_barrier((main, over))
    return exchange(main), over


def share_total_kernel(incoming, out):
    total = incoming[0].astype(F32)
    for r in range(1, incoming.shape[0]):
        total = total + incoming[r].astype(F32)
    out[...] = total


def share_total(returned):
    rows = returned.shape[0]
    return pl.pallas_call(
        share_total_kernel,
        grid=(1,),
        in_specs=[pl.BlockSpec((rows, EDGE, 128), lambda i: (0, 0, 0))],
        out_specs=pl.BlockSpec((EDGE, 128), lambda i: (0, 0)),
        out_shape=jax.ShapeDtypeStruct((EDGE, 128), F32),
        compiler_params=params(),
    )(returned)


def share_sum(piece, parts, rows):
    row = lax.axis_index("rows")
    have = [piece] + [
        lax.ppermute(piece, "rows", [(i, i ^ k) for i in range(rows)]) for k in range(1, parts)
    ]
    bit = 1
    while bit < parts:
        odd = (row & bit) > 0
        have = [jnp.where(odd, have[i ^ bit], have[i]) for i in range(parts)]
        bit *= 2
    return have


def on_device(features, weight, cotangent, blocks, row_block, src_owner, src_block, live):
    rows = lax.axis_size("rows")
    feats = lax.axis_size("feat")
    me = lax.axis_index("feat")
    width, nodes = features.shape
    size = blocks.shape[2]
    slots = blocks.shape[1]
    local = nodes // size
    most = max(2, 2 * slots // rows) * feats
    extra = EXTRA
    main = most - extra
    head = HEAD

    own_tiles = blocks[0]
    far_head = chip_swap(own_tiles[:head])

    here = jnp.arange(slots, dtype=I32)
    alive = here < live[0, 0]
    code = jnp.where(alive, src_owner[0, :, 0] * 64 + src_block[0], -1)
    goal = jnp.where(alive, row_block[0], local)
    note = gather_feat(jnp.stack([code, goal]))
    code = jnp.concatenate([n[0] for n in note])
    target = jnp.concatenate([n[1] for n in note])
    valid = code >= 0
    owner = jnp.where(valid, code >> 6, -1)
    block = jnp.where(valid, code & 63, -1)
    owner_hot = owner[:, None] == jnp.arange(rows, dtype=I32)[None, :]
    block_hot = block[:, None] == jnp.arange(local, dtype=I32)[None, :]
    want = exact_dot(owner_hot.T, block_hot) > 0.5
    rank = ranks(want)
    largest = jnp.max(jnp.sum(want.astype(I32), axis=1))
    request = jnp.concatenate(
        [want.astype(I32), jnp.broadcast_to(largest, (rows, 128 - local))], axis=1
    )
    weights = relative(jnp.concatenate(gather_feat(weight), axis=0), 1, me)

    slot_rank = jnp.sum(jnp.where(block_hot, exact_dot(owner_hot, rank), 0.0), axis=1).astype(I32)
    place = jnp.where(valid, owner * 64 + slot_rank, rows * 64)
    order = jnp.arange(feats * slots, dtype=I32)
    again = jnp.any(
        (code[:, None] == code[None, :]) & (order[None, :] < order[:, None]), axis=1
    ).astype(I32)
    counts = jnp.sum(valid.astype(I32).reshape(feats, slots), axis=1)
    answer = exchange(request)
    answer, far_head, weights, place, again, counts, target = lax.optimization_barrier(
        (answer, far_head, weights, place, again, counts, target)
    )
    asked = answer[:, :local]
    needed = jnp.max(answer[:, local]) > main
    asked_rank = ranks(asked)
    asked_count = jnp.sum(asked, axis=1)
    at = jnp.arange(STRIDE, dtype=I32)[None, :, None]
    chosen = (asked[:, None, :] > 0) & (asked_rank[:, None, :] == at)
    index = local + jnp.sum(jnp.where(chosen, jnp.arange(local, dtype=I32) - local, 0), axis=2)
    served, over = serve(features, index, asked_count, rows, main, extra)
    panels, over = exchange_both(served, over, needed)
    panels = panels.reshape(rows, main, width, size)
    over = over.reshape(rows, extra, width, size)

    far_tail, cotangent, answer = lax.optimization_barrier((own_tiles[head:], cotangent, answer))
    far_tail = chip_swap(far_tail)
    tiles = (
        own_tiles,
        core_swap(own_tiles),
        far_head,
        far_tail,
        core_swap(far_head),
        core_swap(far_tail),
    )
    lists = (
        feats,
        (
            ((0, 0, slots),),
            ((1, 0, slots),),
            ((2, 0, head), (3, head, slots - head)),
            ((4, 0, head), (5, head, slots - head)),
        ),
    )
    cotangents = gather_feat(cotangent)
    flag = needed.astype(I32).reshape(1)

    own = aggregate(panels, over, tiles, lists, slots, place, target, counts, flag, local)
    aggregated = gather_feat(own)
    activation, grads, shares = middle(weights, aggregated, cotangents)
    made, over = terms(
        grads, shares, tiles, lists, slots, place, target, again, counts, rows, main, extra
    )
    returned, over = exchange_both(made, over, needed)
    piece = share_total(returned)
    total = jnp.concatenate(share_sum(piece, shares.shape[0] // EDGE, rows), axis=0)
    total = jnp.concatenate(jnp.split(total, total.shape[0] // width, axis=0), axis=1)
    weight_grad = relative(total, 1, me) * (1.0 / math.sqrt(nodes * rows))
    feature_grad = collect(returned, over, index, asked_count, local, width, main, extra)
    return (activation, feature_grad, weight_grad)


def solution(mesh):
    placed = (
        P("feat", "rows"),
        P("feat", None),
        P("feat", "rows"),
        P("rows", "feat", None, None),
        P("rows", "feat"),
        P("rows", "feat", None),
        P("rows", "feat"),
        P("rows", "feat"),
    )
    return jax.shard_map(
        on_device,
        mesh=mesh,
        in_specs=placed,
        out_specs=(P("feat", "rows"), P("feat", "rows"), P("feat", None)),
        check_vma=False,
    )
```

profile of v0, /device:TPU:0, one launch (start us, length us, event | category | flops | bytes accessed | tf_op | source)
XLA Modules:
  0.0 330.4 jit_solution(5656192245065000625)
XLA Ops:
  1.3 0.7 compare_select_fusion
  2.0 2.1 collective-permute-start.1
  4.1 0.2 collective-permute-start.5
  4.3 0.3 collective-permute-start.4
  4.6 1.4 slice_bitcast_fusion
  6.0 1.8 collective-permute-start.3
  8.1 1.1 collective-permute-done.2
  9.3 0.3 fusion.15
  9.6 0.6 reduce_max.18
  10.3 1.3 concatenate.48
  11.5 10.3 %all-to-all-start.2 = ((s32[32,1,128]{2,1,0:T(1,128)}), s32[32,1,128]{2,1,0:T(1,128)S(1)}, u32[]{:S(2)}, u32[]{:S(2)}) async-start(s32[32,1,128]{2,1,0:T(1,128)} %bitcast.8), calls=%async_computation.2 | async-start | bytes 32768 | tf_op jit(solution)/shard_map/all_to_all | solution.py:408
  21.9 0.3 fusion
  22.4 0.6 add_select_fusion.place
  23.0 0.7 pad_add_fusion.2.target
  23.6 0.6 convert_element_type.44.again
  24.3 0.7 reduce_sum.47.live
  25.0 1.2 collective-permute-done.6
  26.3 0.8 pad_maximum_fusion.weight
  27.1 13.5 %all-to-all-done.2 = s32[32,1,128]{2,1,0:T(1,128)S(1)} async-done(((s32[32,1,128]{2,1,0:T(1,128)}), s32[32,1,128]{2,1,0:T(1,128)S(1)}, u32[]{:S(2)}, u32[]{:S(2)}) %all-to-all-start.2) | async-done | bytes 16416 | tf_op jit(solution)/shard_map/all_to_all | solution.py:408
  40.7 0.8 slice_reduce_fusion.1.count
  41.5 0.7 slice_reduce_fusion
  42.2 0.6 select_reduce_fusion
  42.8 0.6 broadcast_add_fusion.index
  44.1 7.6 %shard_map.103 = (bf16[32,896,128]{2,1,0:T(8,128)(2,1)}, bf16[32,128,128]{2,1,0:T(8,128)(2,1)S(1)}) custom-call(s32[32,16]{1,0:T(8,128)} %broadcast_add_fusion.index, s32[32]{0:T(128)} %slice_reduce_fusion.1.count, bf16[64,6144]{1,0:T(8,128)(2,1)} %features.1), custom_call_target="tpu_custom_call" | custom-call | bytes 8388608 | tf_op jit(solution)/shard_map/pallas_call | solution.py:87
  51.7 1.0 copy-done.4
  52.7 7.7 %all-to-all-start.3 = ((bf16[32,896,128]{2,1,0:T(8,128)(2,1)}), bf16[32,896,128]{2,1,0:T(8,128)(2,1)}, u32[]{:S(2)}, u32[]{:S(2)}) async-start(bf16[32,896,128]{2,1,0:T(8,128)(2,1)} %get-tuple-element.40), calls=%async_computation.3 | async-start | bytes 14680064 | tf_op jit(solution)/shard_map/all_to_all | solution.py:408
  60.6 0.8 collective-permute-start.8
  61.4 0.2 collective-permute-start.9
  61.6 95.3 %collective-permute-done.8.refs_3_ = bf16[24,128,128]{2,1,0:T(8,128)(2,1)S(1)} collective-permute-done((bf16[24,128,128]{2,1,0:T(8,128)(2,1)S(1)}, bf16[24,128,128]{2,1,0:T(8,128)(2,1)S(1)}, u32[]{:S(2)}, u32[]{:S(2)}) %collective-permute-start.8) | collective-permute-done | bytes 786464 | tf_op jit(solution)/shard_map/ppermute | solution.py:32
  156.9 1.0 collective-permute-start.15
  157.9 1.3 copy-done.1
  159.2 1.1 copy-done.3
  160.3 12.2 %shard_map.104.a0 = bf16[48,64,128]{2,1,0:T(8,128)(2,1)} custom-call(s32[256]{0:T(256)} %add_select_fusion.place, s32[256]{0:T(256)} %pad_add_fusion.2.target, s32[4]{0:T(128)} %reduce_sum.47.live, s32[1]{0:T(128)} %bitcast.15.flag, bf16[32,14,64,128]{3,2,1,0:T(8,128)(2,1)} %bitcast.16.panels, bf16[32,2,64,128]{3,2,1,0:T(8,128)(2,1)} %bitcast.44, ...), custom_call_target="tpu_custom_call" | custom-call | flops 536870912 | bytes 15728640 | tf_op jit(solution)/shard_map/pallas_call | solution.py:179
  172.5 1.1 collective-permute-start.12
  173.6 3.9 %collective-permute-done.15.c2 = bf16[64,6144]{1,0:T(8,128)(2,1)} collective-permute-done((bf16[64,6144]{1,0:T(8,128)(2,1)}, bf16[64,6144]{1,0:T(8,128)(2,1)}, u32[]{:S(2)}, u32[]{:S(2)}) %collective-permute-start.15) | collective-permute-done | bytes 786464 | tf_op jit(solution)/shard_map/ppermute | solution.py:32
  177.6 0.5 collective-permute-start.11
  178.1 15.9 %collective-permute-done.12.a2 = bf16[48,64,128]{2,1,0:T(8,128)(2,1)S(1)} collective-permute-done((bf16[48,64,128]{2,1,0:T(8,128)(2,1)}, bf16[48,64,128]{2,1,0:T(8,128)(2,1)S(1)}, u32[]{:S(2)}, u32[]{:S(2)}) %collective-permute-start.12) | collective-permute-done | bytes 786464 | tf_op jit(solution)/shard_map/ppermute | solution.py:32
  194.0 2.2 collective-permute-done.13.a3
  196.2 0.9 copy-done.11
  197.1 8.2 %shard_map.105 = (bf16[64,6144]{1,0:T(8,128)(2,1)}, bf16[48,64,128]{2,1,0:T(8,128)(2,1)}, bf16[128,128]{1,0:T(8,128)(2,1)}) custom-call(bf16[256,256]{1,0:T(8,128)(2,1)} %pad_maximum_fusion.weight, bf16[48,64,128]{2,1,0:T(8,128)(2,1)} %shard_map.104.a0, bf16[48,64,128]{2,1,0:T(8,128)(2,1)} %copy-done.10, bf16[48,64,128]{2,1,0:T(8,128)(2,1)} %copy-done.7, ...), custom_call_target="tpu_custom_call" | custom-call | flops 1207959552 | bytes 7864320 | tf_op jit(solution)/shard_map/pallas_call | solution.py:246
  205.3 11.5 %shard_map.106 = (bf16[32,928,128]{2,1,0:T(8,128)(2,1)}, bf16[32,128,128]{2,1,0:T(8,128)(2,1)S(1)}) custom-call(s32[256]{0:T(256)} %add_select_fusion.place, s32[256]{0:T(256)} %pad_add_fusion.2.target, s32[256]{0:T(256)} %convert_element_type.44.again, s32[4]{0:T(128)} %reduce_sum.47.live, bf16[48,64,128]{2,1,0:T(8,128)(2,1)} %get-tuple-element.47.grads, ...), custom_call_target="tpu_custom_call" | custom-call | flops 536870912 | bytes 15728640 | tf_op jit(solution)/shard_map/pallas_call | solution.py:318
  216.9 98.4 %all_to_all.32.incoming = bf16[32,928,128]{2,1,0:T(8,128)(2,1)} all-to-all(bf16[32,928,128]{2,1,0:T(8,128)(2,1)} %get-tuple-element.51), channel_id=1, replica_groups=mesh['rows'=32,'feat'=4] {'rows'}, dimensions={0} | all-to-all | bytes 15204352 | tf_op jit(solution)/shard_map/all_to_all | solution.py:408
  315.2 1.6 shard_map.108
  316.9 0.4 collective-permute-start.17
  317.2 1.3 collective-permute-start.18
  318.6 2.4 collective-permute-start.19
  321.0 8.6 %shard_map.107 = bf16[64,6144]{1,0:T(8,128)(2,1)} custom-call(s32[32,16]{1,0:T(8,128)} %broadcast_add_fusion.index, s32[32]{0:T(128)} %slice_reduce_fusion.1.count, bf16[32,928,128]{2,1,0:T(8,128)(2,1)} %all_to_all.32.incoming, bf16[32,128,128]{2,1,0:T(8,128)(2,1)S(1)} %get-tuple-element.82.over), custom_call_target="tpu_custom_call" | custom-call | flops 3670016 | bytes 7340032 | tf_op jit(solution)/shard_map/pallas_call | solution.py:385
  329.7 0.7 maximum_multiply_fusion
  (78 shorter events, 1.2 us)
Async XLA Ops:
  0.6 7.3 %copy-start.16 = (s32[1,64]{1,0:T(1,128)S(1)}, s32[1,64]{1,0:T(1,128)}, u32[]{:S(2)}) copy-start(s32[1,64]{1,0:T(1,128)} %param.16) | copy-start | bytes 772
  0.6 7.2 %copy-start.15 = (s32[1,64,1]{1,2,0:T(1,128)S(1)}, s32[1,64,1]{1,2,0:T(1,128)}, u32[]{:S(2)}) copy-start(s32[1,64,1]{1,2,0:T(1,128)} %param.17) | copy-start | bytes 772
  0.7 7.2 %copy-start.14 = (s32[1,64]{1,0:T(1,128)S(1)}, s32[1,64]{1,0:T(1,128)}, u32[]{:S(2)}) copy-start(s32[1,64]{1,0:T(1,128)} %param.18) | copy-start | bytes 772
  0.7 7.2 %copy-start.13 = (bf16[64,256]{1,0:T(8,128)(2,1)S(1)}, bf16[64,256]{1,0:T(8,128)(2,1)}, u32[]{:S(2)}) copy-start(bf16[64,256]{1,0:T(8,128)(2,1)} %param.13) | copy-start | bytes 98308
  2.0 5.9 %collective-permute-start.1 = (s32[2,64]{1,0:T(2,128)S(1)}, s32[2,64]{1,0:T(2,128)S(1)}, u32[]{:S(2)}, u32[]{:S(2)}) collective-permute-start(s32[2,64]{1,0:T(2,128)S(1)} %pad_add_fusion), channel_id=1, source_target_pairs={{0,2},{2,0},{1,3},{3,1},{4,6},{6,4},{5,7},{7,5},{8,10},{10,8},{9,1... | collective-permute-start | bytes 1544 | tf_op jit(solution)/shard_map/ppermute | solution.py:32
  4.1 3.9 %collective-permute-start = (s32[2,64]{1,0:T(2,128)S(1)}, s32[2,64]{1,0:T(2,128)S(1)}, u32[]{:S(2)}, u32[]{:S(2)}) collective-permute-start(s32[2,64]{1,0:T(2,128)S(1)} %pad_add_fusion), channel_id=1, source_target_pairs={{0,1},{1,0},{2,3},{3,2},{4,5},{5,4},{6,7},{7,6},{8,9},{9,8},{10,11... | collective-permute-start | bytes 1544 | tf_op jit(solution)/shard_map/ppermute | solution.py:28
  4.1 20.8 %collective-permute-start.5 = (bf16[64,256]{1,0:T(8,128)(2,1)}, bf16[64,256]{1,0:T(8,128)(2,1)S(1)}, u32[]{:S(2)}, u32[]{:S(2)}) collective-permute-start(bf16[64,256]{1,0:T(8,128)(2,1)} %param.13), channel_id=1, source_target_pairs={{0,2},{2,0},{1,3},{3,1},{4,6},{6,4},{5,7},{7,5},{8,10},{10,8},{9,1... | collective-permute-start | bytes 98312 | tf_op jit(solution)/shard_map/ppermute | solution.py:32
  4.3 20.7 %collective-permute-start.4 = (bf16[64,256]{1,0:T(8,128)(2,1)}, bf16[64,256]{1,0:T(8,128)(2,1)S(1)}, u32[]{:S(2)}, u32[]{:S(2)}) collective-permute-start(bf16[64,256]{1,0:T(8,128)(2,1)} %param.13), channel_id=1, source_target_pairs={{0,1},{1,0},{2,3},{3,2},{4,5},{5,4},{6,7},{7,6},{8,9},{9,8},{10,11... | collective-permute-start | bytes 98312 | tf_op jit(solution)/shard_map/ppermute | solution.py:28
  6.0 34.5 %collective-permute-start.3 = (bf16[40,128,128]{2,1,0:T(8,128)(2,1)S(1)}, bf16[40,128,128]{2,1,0:T(8,128)(2,1)S(1)}, u32[]{:S(2)}, u32[]{:S(2)}) collective-permute-start(bf16[40,128,128]{2,1,0:T(8,128)(2,1)S(1)} %slice_bitcast_fusion), channel_id=1, source_target_pairs={{0,2},{2,0},{1,3},{3,1},{4,6},{6,4},{5,7},{7,5},{8,10},{10,8},{9,1... | collective-permute-start | bytes 3932168 | tf_op jit(solution)/shard_map/ppermute | solution.py:32
  8.0 1.2 collective-permute-start.2
  11.5 29.0 %all-to-all-start.2 = ((s32[32,1,128]{2,1,0:T(1,128)}), s32[32,1,128]{2,1,0:T(1,128)S(1)}, u32[]{:S(2)}, u32[]{:S(2)}) async-start(s32[32,1,128]{2,1,0:T(1,128)} %bitcast.8), calls=%async_computation.2 | async-start | bytes 32768 | tf_op jit(solution)/shard_map/all_to_all | solution.py:408
  25.0 1.2 collective-permute-start.6
  40.5 20.9 %copy-start.2 = (bf16[40,128,128]{2,1,0:T(8,128)(2,1)}, bf16[40,128,128]{2,1,0:T(8,128)(2,1)S(1)}, u32[]{:S(2)}) copy-start(bf16[40,128,128]{2,1,0:T(8,128)(2,1)S(1)} %collective-permute-done.3.refs_2_) | copy-start | bytes 3932164
  51.7 1.0 copy-start.4
  52.7 7.7 %copy-start = (bf16[1,64,128,128]{3,2,1,0:T(8,128)(2,1)S(1)}, bf16[1,64,128,128]{3,2,1,0:T(8,128)(2,1)}, u32[]{:S(2)}) copy-start(bf16[1,64,128,128]{3,2,1,0:T(8,128)(2,1)} %param.15) | copy-start | bytes 6291460
  52.7 107.6 %all-to-all-start.3 = ((bf16[32,896,128]{2,1,0:T(8,128)(2,1)}), bf16[32,896,128]{2,1,0:T(8,128)(2,1)}, u32[]{:S(2)}, u32[]{:S(2)}) async-start(bf16[32,896,128]{2,1,0:T(8,128)(2,1)} %get-tuple-element.40), calls=%async_computation.3 | async-start | bytes 14680064 | tf_op jit(solution)/shard_map/all_to_all | solution.py:408
  60.4 97.5 %collective-permute-start.7 = (bf16[64,128,128]{2,1,0:T(8,128)(2,1)S(1)}, bf16[64,128,128]{2,1,0:T(8,128)(2,1)S(1)}, u32[]{:S(2)}, u32[]{:S(2)}) collective-permute-start(bf16[64,128,128]{2,1,0:T(8,128)(2,1)S(1)} %bitcast.43), channel_id=1, source_target_pairs={{0,1},{1,0},{2,3},{3,2},{4,5},{5,4},{6,7},{7,6},{8,9},{9,8},{10,11... | collective-permute-start | bytes 6291464 | tf_op jit(solution)/shard_map/ppermute | solution.py:28
  60.6 96.3 %collective-permute-start.8 = (bf16[24,128,128]{2,1,0:T(8,128)(2,1)S(1)}, bf16[24,128,128]{2,1,0:T(8,128)(2,1)S(1)}, u32[]{:S(2)}, u32[]{:S(2)}) collective-permute-start(bf16[24,128,128]{2,1,0:T(8,128)(2,1)S(1)} %slice_bitcast_fusion.1), channel_id=1, source_target_pairs={{0,2},{2,0},{1,3},{3,1},{4,6},{6,4},{5,7},{7,5},{8,10},{10,8},{9,1... | collective-permute-start | bytes 2359304 | tf_op jit(solution)/shard_map/ppermute | solution.py:32
  61.4 97.8 %collective-permute-start.9 = (bf16[40,128,128]{2,1,0:T(8,128)(2,1)S(1)}, bf16[40,128,128]{2,1,0:T(8,128)(2,1)S(1)}, u32[]{:S(2)}, u32[]{:S(2)}) collective-permute-start(bf16[40,128,128]{2,1,0:T(8,128)(2,1)S(1)} %collective-permute-done.3.refs_2_), channel_id=1, source_target_pairs={{0,1},{1,0},{2,3},{3,2},{4,5},{5,4},{6,7},{7,6},{8,9},{9,8},{10,11... | collective-permute-start | bytes 3932168 | tf_op jit(solution)/shard_map/ppermute | solution.py:28
  156.9 2.3 copy-start.5
  156.9 3.4 %collective-permute-start.10 = (bf16[24,128,128]{2,1,0:T(8,128)(2,1)S(1)}, bf16[24,128,128]{2,1,0:T(8,128)(2,1)}, u32[]{:S(2)}, u32[]{:S(2)}) collective-permute-start(bf16[24,128,128]{2,1,0:T(8,128)(2,1)S(1)} %collective-permute-done.8.refs_3_), channel_id=1, source_target_pairs={{0,1},{1,0},{2,3},{3,2},{4,5},{5,4},{6,7},{7,6},{8,9},{9,8},{10,11... | collective-permute-start | bytes 2359304 | tf_op jit(solution)/shard_map/ppermute | solution.py:28
  156.9 20.7 %collective-permute-start.15 = (bf16[64,6144]{1,0:T(8,128)(2,1)}, bf16[64,6144]{1,0:T(8,128)(2,1)}, u32[]{:S(2)}, u32[]{:S(2)}) collective-permute-start(bf16[64,6144]{1,0:T(8,128)(2,1)} %c0), channel_id=1, source_target_pairs={{0,2},{2,0},{1,3},{3,1},{4,6},{6,4},{5,7},{7,5},{8,10},{10,8},{9,1... | collective-permute-start | bytes 2359304 | tf_op jit(solution)/shard_map/ppermute | solution.py:32
  157.9 1.3 copy-start.1
  159.2 1.1 copy-start.3
  160.3 13.3 %copy-start.6 = (bf16[64,6144]{1,0:T(8,128)(2,1)S(1)}, bf16[64,6144]{1,0:T(8,128)(2,1)}, u32[]{:S(2)}) copy-start(bf16[64,6144]{1,0:T(8,128)(2,1)} %c0) | copy-start | bytes 2359300
  172.5 21.4 %collective-permute-start.12 = (bf16[48,64,128]{2,1,0:T(8,128)(2,1)}, bf16[48,64,128]{2,1,0:T(8,128)(2,1)S(1)}, u32[]{:S(2)}, u32[]{:S(2)}) collective-permute-start(bf16[48,64,128]{2,1,0:T(8,128)(2,1)} %shard_map.104.a0), channel_id=1, source_target_pairs={{0,2},{2,0},{1,3},{3,1},{4,6},{6,4},{5,7},{7,5},{8,10},{10,8},{9,1... | collective-permute-start | bytes 2359304 | tf_op jit(solution)/shard_map/ppermute | solution.py:32
  173.6 20.3 %collective-permute-start.14 = (bf16[64,6144]{1,0:T(8,128)(2,1)S(1)}, bf16[64,6144]{1,0:T(8,128)(2,1)S(1)}, u32[]{:S(2)}, u32[]{:S(2)}) collective-permute-start(bf16[64,6144]{1,0:T(8,128)(2,1)S(1)} %copy-done.6), channel_id=1, source_target_pairs={{0,1},{1,0},{2,3},{3,2},{4,5},{5,4},{6,7},{7,6},{8,9},{9,8},{10,11... | collective-permute-start | bytes 2359304 | tf_op jit(solution)/shard_map/ppermute | solution.py:28
  177.5 16.4 %collective-permute-start.16 = (bf16[64,6144]{1,0:T(8,128)(2,1)}, bf16[64,6144]{1,0:T(8,128)(2,1)S(1)}, u32[]{:S(2)}, u32[]{:S(2)}) collective-permute-start(bf16[64,6144]{1,0:T(8,128)(2,1)} %collective-permute-done.15.c2), channel_id=1, source_target_pairs={{0,1},{1,0},{2,3},{3,2},{4,5},{5,4},{6,7},{7,6},{8,9},{9,8},{10,11... | collective-permute-start | bytes 2359304 | tf_op jit(solution)/shard_map/ppermute | solution.py:28
  177.6 16.4 %collective-permute-start.11 = (bf16[48,64,128]{2,1,0:T(8,128)(2,1)}, bf16[48,64,128]{2,1,0:T(8,128)(2,1)S(1)}, u32[]{:S(2)}, u32[]{:S(2)}) collective-permute-start(bf16[48,64,128]{2,1,0:T(8,128)(2,1)} %shard_map.104.a0), channel_id=1, source_target_pairs={{0,1},{1,0},{2,3},{3,2},{4,5},{5,4},{6,7},{7,6},{8,9},{9,8},{10,11... | collective-permute-start | bytes 2359304 | tf_op jit(solution)/shard_map/ppermute | solution.py:28
  193.9 2.3 copy-start.7
  193.9 2.3 collective-permute-start.13
  193.9 2.3 copy-start.8
  193.9 2.3 copy-start.9
  194.0 2.2 copy-start.10
  196.2 0.9 copy-start.11
  316.9 12.7 %collective-permute-start.17 = (f32[32,128]{1,0:T(8,128)}, f32[32,128]{1,0:T(8,128)S(1)}, u32[]{:S(2)}, u32[]{:S(2)}) collective-permute-start(f32[32,128]{1,0:T(8,128)} %shard_map.108), channel_id=1, source_target_pairs={{0,4},{4,0},{8,12},{12,8},{16,20},{20,16},{24,28},{28,24},{32,36},... | collective-permute-start | bytes 49160 | tf_op jit(solution)/shard_map/ppermute | solution.py:439
  317.2 12.3 %collective-permute-start.18 = (f32[32,128]{1,0:T(8,128)}, f32[32,128]{1,0:T(8,128)S(1)}, u32[]{:S(2)}, u32[]{:S(2)}) collective-permute-start(f32[32,128]{1,0:T(8,128)} %shard_map.108), channel_id=1, source_target_pairs={{0,12},{4,8},{8,4},{12,0},{16,28},{20,24},{24,20},{28,16},{32,44},... | collective-permute-start | bytes 49160 | tf_op jit(solution)/shard_map/ppermute | solution.py:439
  318.6 11.0 %collective-permute-start.19 = (f32[32,128]{1,0:T(8,128)}, f32[32,128]{1,0:T(8,128)S(1)}, u32[]{:S(2)}, u32[]{:S(2)}) collective-permute-start(f32[32,128]{1,0:T(8,128)} %shard_map.108), channel_id=1, source_target_pairs={{0,8},{4,12},{8,0},{12,4},{16,24},{20,28},{24,16},{28,20},{32,40},... | collective-permute-start | bytes 49160 | tf_op jit(solution)/shard_map/ppermute | solution.py:439
  320.9 8.6 %copy-start.12 = (f32[32,128]{1,0:T(8,128)S(1)}, f32[32,128]{1,0:T(8,128)}, u32[]{:S(2)}) copy-start(f32[32,128]{1,0:T(8,128)} %shard_map.108) | copy-start | bytes 49156
where the time goes:
time: 332 us; the launch traced here: 330 us
  waiting for transfers between devices  133 us (40%)
  blocking collectives  98.4 us (30%)
  Pallas kernels  49.7 us (15%)
  starting transfers between devices  30.4 us (9%)
  other arithmetic  8.73 us (3%)
  local copies, waits for them, and re-layouts  7.14 us (2%)
    ppermute x6, waiting for transfers between devices, chip_swap(): return lax.ppermute(x, 'feat', [(0, 2), (2, 0), (1, 3), (3, 1)])  115 us
    all_to_all x1, blocking collectives, exchange(): return lax.all_to_all(x, 'rows', split_axis=0, concat_axis=0, tiled=True)  98.4 us
    all_to_all x2, starting transfers between devices, exchange(): return lax.all_to_all(x, 'rows', split_axis=0, concat_axis=0, tiled=True)  18 us
    all_to_all x2, waiting for transfers between devices, exchange(): return lax.all_to_all(x, 'rows', split_axis=0, concat_axis=0, tiled=True)  13.5 us
    pallas_call x1, Pallas kernels, aggregate(): pl.pallas_call(functools.partial(aggregate_kernel, lists, slots), grid_sp...  12.2 us
    pallas_call x1, Pallas kernels, terms(): pl.pallas_call(functools.partial(terms_kernel, lists, slots), grid_spec=p...  11.5 us
    pallas_call x1, Pallas kernels, collect(): pl.pallas_call(functools.partial(collect_kernel, step, blocks, main), gri...  8.56 us
    pallas_call x1, Pallas kernels, middle(): pl.pallas_call(functools.partial(middle_kernel, step), grid=(blocks // st...  8.18 us
  transfers between devices with their start and end apart: 22, of which 7 were waited for; matrix products, arithmetic and copies ran while one was open for 2% of the time, Pallas kernels for 6%

commit v1 on v0

--- a/solution.py
+++ b/solution.py
@@ -14,7 +14,6 @@
 VMEM_LIMIT = 56 * 1024 * 1024
 GROUP = 8
 STRIDE = 16
-UNROLL = 7
 EDGE = 32
 EXTRA = 2
 HEAD = 40
@@ -56,43 +55,61 @@
     return exact_dot(want, upper).astype(I32)
 
 
-def serve_kernel(step, main, index, count, features, out, over):
+def each_row(rows, first, act):
+    def body(r, carry):
+        act(r)
+        return carry
+
+    lax.fori_loop(first, rows, body, 0)
+
+
+def serve_kernel(spans, index, count, features, out, over, buf, sems):
     width = features.shape[0]
-    for i in range(step):
-        row = pl.program_id(0) * step + i
-
-        def put(ref, first, k):
-            block = jnp.minimum(index[row, k], features.shape[1] // 128 - 1)
+    rows = out.shape[0]
+    main = spans[-1][0]
+
+    def sent(r, n):
+        low, high = spans[n]
+        ref, base = (over, main) if low >= main else (out, 0)
+        return pltpu.make_async_copy(
+            buf.at[r, pl.ds(low * width, (high - low) * width)],
+            ref.at[r, pl.ds((low - base) * width, (high - low) * width)],
+            sems.at[r, n],
+        )
+
+    def fill(r, n):
+        for k in range(*spans[n]):
+            block = jnp.minimum(index[r, k], features.shape[1] // 128 - 1)
             start = pl.multiple_of(block * 128, 128)
-            to = pl.multiple_of((k - first) * width, width)
-            ref[i, pl.ds(to, width), :] = features[:, pl.ds(start, 128)]
-
-        def body(g, carry):
-            for u in range(UNROLL):
-                put(out, 0, g * UNROLL + u)
-            return carry
-
-        lax.fori_loop(0, (jnp.minimum(count[row], main) + UNROLL - 1) // UNROLL, body, 0)
-
-        @pl.when(count[row] > main)
-        def _():
-            for k in range(main, main + over.shape[1] // width):
-                put(over, main, k)
+            buf[r, k * width : (k + 1) * width, :] = features[:, pl.ds(start, 128)]
+        sent(r, n).start()
+
+    def spread(act):
+        def body(r):
+            act(r, 0)
+            for n in (1, 2):
+                pl.when(count[r] > spans[n][0])(functools.partial(act, r, n))
+
+        each_row(rows, 0, body)
+
+    spread(fill)
+    spread(lambda r, n: sent(r, n).wait())
 
 
 def serve(features, index, count, rows, main, extra):
     width, nodes = features.shape
-    step = 4
-    place = lambda r, *_: (r, 0, 0)
+    any_spec = pl.BlockSpec(memory_space=pl.ANY)
+    spans = ((0, main // 2), (main // 2, main), (main, main + extra))
     return pl.pallas_call(
-        functools.partial(serve_kernel, step, main),
+        functools.partial(serve_kernel, spans),
         grid_spec=pltpu.PrefetchScalarGridSpec(
             num_scalar_prefetch=2,
-            grid=(rows // step,),
+            grid=(1,),
             in_specs=[pl.BlockSpec((width, nodes), lambda r, *_: (0, 0))],
-            out_specs=[
-                pl.BlockSpec((step, main * width, 128), place),
-                pl.BlockSpec((step, extra * width, 128), place),
+            out_specs=[any_spec, any_spec],
+            scratch_shapes=[
+                pltpu.VMEM((rows, (main + extra) * width, 128), BF),
+                pltpu.SemaphoreType.DMA((rows, 3)),
             ],
         ),
         out_shape=[
@@ -121,29 +138,45 @@
     return copies
 
 
-def aggregate_kernel(lists, slots, place, target, live, flag, panels, over, *refs):
+def aggregate_kernel(lists, slots, place, target, live, used, panels, over, *refs):
     pieces = sum(len(x) for x in lists[1])
     tiles = refs[:pieces]
-    out, held, panel, acc, sems = refs[pieces:]
+    out, held, panel, acc, sems, row_sems = refs[pieces:]
     blocks = out.shape[0]
     rows, main = panels.shape[:2]
     extra = over.shape[1]
-    first = pltpu.make_async_copy(panels, panel.at[pl.ds(0, rows), pl.ds(0, main)], sems.at[pieces])
+    half = main // 2
+    first = pltpu.make_async_copy(
+        panels.at[:, pl.ds(0, half)], panel.at[pl.ds(0, rows), pl.ds(0, half)], sems.at[pieces]
+    )
     first.start()
+
+    def late(r):
+        return pltpu.make_async_copy(
+            panels.at[r, pl.ds(half, main - half)],
+            panel.at[r, pl.ds(half, main - half)],
+            row_sems.at[r, 0],
+        )
+
+    def more(r):
+        return pltpu.make_async_copy(over.at[r], panel.at[r, pl.ds(main, extra)], row_sems.at[r, 1])
+
+    def start(r):
+        pl.when(used[r] > half)(lambda: late(r).start())
+        pl.when(used[r] > main)(lambda: more(r).start())
+
+    def finish(r):
+        pl.when(used[r] > half)(lambda: late(r).wait())
+        pl.when(used[r] > main)(lambda: more(r).wait())
+
+    each_row(rows, 0, start)
     copies = tile_copies(lists, tiles, held, sems)
     for group in copies:
         for c in group:
             c.start()
     acc[...] = jnp.zeros_like(acc)
 
-    @pl.when(flag[0] > 0)
-    def _():
-        more = pltpu.make_async_copy(
-            over, panel.at[pl.ds(0, rows), pl.ds(main, extra)], sems.at[pieces + 1]
-        )
-        more.start()
-        more.wait()
-
+    each_row(rows, 0, finish)
     first.wait()
     for j in range(lists[0]):
         for c in copies[j]:
@@ -164,14 +197,15 @@
                 )
             for u in range(GROUP):
                 t = target[j * slots + base + u]
-                acc[t] = acc[t] + products[u]
+                acc[u % 2, t] = acc[u % 2, t] + products[u]
             return carry
 
         lax.fori_loop(0, (live[j] + GROUP - 1) // GROUP, body, 0)
-    out[...] = acc[:blocks].astype(BF)
-
-
-def aggregate(panels, over, tiles, lists, slots, place, target, live, flag, blocks):
+    for t in range(blocks):
+        out[t] = (acc[0, t] + acc[1, t]).astype(BF)
+
+
+def aggregate(panels, over, tiles, lists, slots, place, target, live, used, blocks):
     size = tiles[0].shape[1]
     rows, main, width, _ = panels.shape
     extra = over.shape[1]
@@ -186,8 +220,9 @@
             scratch_shapes=[
                 pltpu.VMEM((lists[0], slots, size, size), BF),
                 pltpu.VMEM((rows + 1, main + extra, width, size), BF),
-                pltpu.VMEM((blocks + 1, width, size), F32),
-                pltpu.SemaphoreType.DMA((len(tiles) + 2,)),
+                pltpu.VMEM((2, blocks + 1, width, size), F32),
+                pltpu.SemaphoreType.DMA((len(tiles) + 1,)),
+                pltpu.SemaphoreType.DMA((rows, 2)),
             ],
         ),
         out_shape=jax.ShapeDtypeStruct((blocks, width, size), BF),
@@ -197,7 +232,7 @@
             bytes_accessed=rows * main * width * size * 2 + lists[0] * slots * size * size * 2,
             transcendentals=0,
         ),
-    )(place, target, live, flag, panels, over, *tiles)
+    )(place, target, live, used, panels, over, *tiles)
 
 
 def middle_kernel(step, weight, a0, a1, a2, a3, c0, c1, c2, c3, act, grad, wgrad, wsum):
@@ -263,10 +298,10 @@
     )(weight, *aggregated, *cotangent)
 
 
-def terms_kernel(lists, slots, place, target, again, live, grads, shares, *refs):
+def terms_kernel(lists, slots, half, place, target, again, live, used, grads, shares, *refs):
     pieces = sum(len(x) for x in lists[1])
     tiles = refs[:pieces]
-    out, over, held, made, sems = refs[pieces:]
+    out, over, held, made, sems, row_sems = refs[pieces:]
     rows, tall = out.shape[:2]
     extra = over.shape[1]
     width = grads.shape[1]
@@ -290,35 +325,66 @@
                 products.append(
                     jnp.dot(grads[t], held[j, base + u], preferred_element_type=F32)
                 )
-            for u in range(GROUP):
+            plain = again[j * slots + base]
+            for u in range(1, GROUP):
+                plain = plain + again[j * slots + base + u]
+
+            def put(u, keep):
                 s = j * slots + base + u
                 at = pl.ds(pl.multiple_of(EDGE + (place[s] & 63) * width, EDGE), width)
                 p = place[s] >> 6
-                kept = jnp.where(again[s] > 0, made[p, at, :].astype(F32), 0.0)
-                made[p, at, :] = (kept + products[u]).astype(BF)
+                value = products[u]
+                if keep:
+                    value = value + jnp.where(again[s] > 0, made[p, at, :].astype(F32), 0.0)
+                made[p, at, :] = value.astype(BF)
+
+            @pl.when(plain == 0)
+            def _():
+                for u in range(GROUP):
+                    put(u, False)
+
+            @pl.when(plain > 0)
+            def _():
+                for u in range(GROUP):
+                    put(u, True)
+
             return carry
 
         lax.fori_loop(0, (live[j] + GROUP - 1) // GROUP, body, 0)
-    last = [
-        pltpu.make_async_copy(made.at[pl.ds(0, rows), pl.ds(0, tall)], out, sems.at[pieces]),
-        pltpu.make_async_copy(
-            made.at[pl.ds(0, rows), pl.ds(tall, extra)], over, sems.at[pieces + 1]
-        ),
-    ]
-    for c in last:
-        c.start()
-    for c in last:
-        c.wait()
-
-
-def terms(grads, shares, tiles, lists, slots, place, target, again, live, rows, main, extra):
+    first = EDGE + half * width
+    whole = pltpu.make_async_copy(
+        made.at[pl.ds(0, rows), pl.ds(0, first)], out.at[:, pl.ds(0, first)], sems.at[pieces]
+    )
+    whole.start()
+
+    def late(r):
+        span = pl.ds(first, tall - first)
+        return pltpu.make_async_copy(made.at[r, span], out.at[r, span], row_sems.at[r, 0])
+
+    def more(r):
+        return pltpu.make_async_copy(made.at[r, pl.ds(tall, extra)], over.at[r], row_sems.at[r, 1])
+
+    def start(r):
+        pl.when(used[r] > half)(lambda: late(r).start())
+        pl.when(used[r] > 2 * half)(lambda: more(r).start())
+
+    def finish(r):
+        pl.when(used[r] > half)(lambda: late(r).wait())
+        pl.when(used[r] > 2 * half)(lambda: more(r).wait())
+
+    each_row(rows, 0, start)
+    each_row(rows, 0, finish)
+    whole.wait()
+
+
+def terms(grads, shares, tiles, lists, slots, place, target, again, live, used, rows, main, extra):
     size = tiles[0].shape[1]
     blocks, width, _ = grads.shape
     any_spec = pl.BlockSpec(memory_space=pl.ANY)
     return pl.pallas_call(
-        functools.partial(terms_kernel, lists, slots),
+        functools.partial(terms_kernel, lists, slots, main // 2),
         grid_spec=pltpu.PrefetchScalarGridSpec(
-            num_scalar_prefetch=4,
+            num_scalar_prefetch=5,
             grid=(1,),
             in_specs=[
                 pl.BlockSpec((blocks, width, size), lambda i, *_: (0, 0, 0)),
@@ -329,7 +395,8 @@
             scratch_shapes=[
                 pltpu.VMEM((lists[0], slots, size, size), BF),
                 pltpu.VMEM((rows + 1, EDGE + (main + extra) * width, size), BF),
-                pltpu.SemaphoreType.DMA((len(tiles) + 2,)),
+                pltpu.SemaphoreType.DMA((len(tiles) + 1,)),
+                pltpu.SemaphoreType.DMA((rows, 2)),
             ],
         ),
         out_shape=[
@@ -342,57 +409,73 @@
             bytes_accessed=rows * main * width * size * 2 + lists[0] * slots * size * size * 2,
             transcendentals=0,
         ),
-    )(place, target, again, live, grads, shares, *tiles)
-
-
-def collect_kernel(step, blocks, main, index, count, incoming, over, out, acc):
+    )(place, target, again, live, used, grads, shares, *tiles)
+
+
+def collect_kernel(chains, spans, blocks, index, count, incoming, over, out, buf, acc, sems):
     width = out.shape[0]
-
-    @pl.when(pl.program_id(0) == 0)
-    def _():
-        acc[...] = jnp.zeros_like(acc)
-
-    for i in range(step):
-        row = pl.program_id(0) * step + i
-
-        def add(ref, shift, k):
-            t = index[row, k]
-            start = pl.multiple_of(k * width + shift, EDGE)
-            acc[t] = acc[t] + ref[i, pl.ds(start, width), :].astype(F32)
-
-        def body(g, carry):
-            for u in range(UNROLL):
-                add(incoming, EDGE, g * UNROLL + u)
-            return carry
-
-        lax.fori_loop(0, (jnp.minimum(count[row], main) + UNROLL - 1) // UNROLL, body, 0)
-
-        @pl.when(count[row] > main)
-        def _():
-            for k in range(main, main + over.shape[1] // width):
-                add(over, -main * width, k)
-
-    @pl.when(pl.program_id(0) == pl.num_programs(0) - 1)
-    def _():
-        for b in range(blocks):
-            out[:, b * 128 : (b + 1) * 128] = acc[b].astype(BF)
+    rows = incoming.shape[0]
+    main = spans[-1][0]
+
+    def came(r, n):
+        low, high = spans[n]
+        if low >= main:
+            source = over.at[r]
+        else:
+            source = incoming.at[r, pl.ds(EDGE + low * width, (high - low) * width)]
+        return pltpu.make_async_copy(
+            source, buf.at[r, pl.ds(low * width, (high - low) * width)], sems.at[r, n]
+        )
+
+    def spread(act, r):
+        act(r, 0)
+        for n in (1, 2):
+            pl.when(count[r] > spans[n][0])(functools.partial(act, r, n))
+
+    each_row(rows, 0, functools.partial(spread, lambda r, n: came(r, n).start()))
+    acc[...] = jnp.zeros_like(acc)
+
+    def add(g, n):
+        for k in range(*spans[n]):
+            for q in range(chains):
+                r = g * chains + q
+                t = index[r, k]
+                acc[q, t] = acc[q, t] + buf[r, k * width : (k + 1) * width, :].astype(F32)
+
+    def body(g):
+        most = count[g * chains]
+        for q in range(chains):
+            spread(lambda r, n: came(r, n).wait(), g * chains + q)
+            most = jnp.maximum(most, count[g * chains + q])
+        add(g, 0)
+        for n in (1, 2):
+            pl.when(most > spans[n][0])(functools.partial(add, g, n))
+
+    each_row(rows // chains, 0, body)
+    for b in range(blocks):
+        total = acc[0, b]
+        for q in range(1, chains):
+            total = total + acc[q, b]
+        out[:, b * 128 : (b + 1) * 128] = total.astype(BF)
 
 
 def collect(incoming, over, index, count, blocks, width, main, extra):
     rows = incoming.shape[0]
-    step = 4
-    place = lambda r, *_: (r, 0, 0)
+    chains = 4
+    any_spec = pl.BlockSpec(memory_space=pl.ANY)
+    spans = ((0, main // 2), (main // 2, main), (main, main + extra))
     return pl.pallas_call(
-        functools.partial(collect_kernel, step, blocks, main),
+        functools.partial(collect_kernel, chains, spans, blocks),
         grid_spec=pltpu.PrefetchScalarGridSpec(
             num_scalar_prefetch=2,
-            grid=(rows // step,),
-            in_specs=[
-                pl.BlockSpec((step, EDGE + main * width, 128), place),
-                pl.BlockSpec((step, extra * width, 128), place),
+            grid=(1,),
+            in_specs=[any_spec, any_spec],
+            out_specs=pl.BlockSpec((width, blocks * 128), lambda r, *_: (0, 0)),
+            scratch_shapes=[
+                pltpu.VMEM((rows, (main + extra) * width, 128), BF),
+                pltpu.VMEM((chains, blocks + 1, width, 128), F32),
+                pltpu.SemaphoreType.DMA((rows, 3)),
             ],
-            out_specs=pl.BlockSpec((width, blocks * 128), lambda r, *_: (0, 0)),
-            scratch_shapes=[pltpu.VMEM((blocks + 1, width, 128), F32)],
         ),
         out_shape=jax.ShapeDtypeStruct((width, blocks * 128), BF),
         compiler_params=params(),
@@ -476,7 +559,8 @@
     block_hot = block[:, None] == jnp.arange(local, dtype=I32)[None, :]
     want = exact_dot(owner_hot.T, block_hot) > 0.5
     rank = ranks(want)
-    largest = jnp.max(jnp.sum(want.astype(I32), axis=1))
+    used = jnp.sum(want.astype(I32), axis=1)
+    largest = jnp.max(used)
     request = jnp.concatenate(
         [want.astype(I32), jnp.broadcast_to(largest, (rows, 128 - local))], axis=1
     )
@@ -525,13 +609,12 @@
         ),
     )
     cotangents = gather_feat(cotangent)
-    flag = needed.astype(I32).reshape(1)
-
-    own = aggregate(panels, over, tiles, lists, slots, place, target, counts, flag, local)
+
+    own = aggregate(panels, over, tiles, lists, slots, place, target, counts, used, local)
     aggregated = gather_feat(own)
     activation, grads, shares = middle(weights, aggregated, cotangents)
     made, over = terms(
-        grads, shares, tiles, lists, slots, place, target, again, counts, rows, main, extra
+        grads, shares, tiles, lists, slots, place, target, again, counts, used, rows, main, extra
     )
     returned, over = exchange_both(made, over, needed)
     piece = share_total(returned)

time: 332 us -> 328 us (0.988)
  Pallas kernels: 49.7 us -> 44.4 us
    pallas_call x3, Pallas kernels: 27.7 us -> 22.8 us  [the longest x1 11.4 us: terms(): pl.pallas_call(functools.partial(terms_kernel, lists, slots, main // 2),...]
  transfers between devices with their start and end apart: 22 -> 22, of which waited for: 7 -> 7; matrix products, arithmetic and copies ran while one was open for 2% -> 2% of each run, Pallas kernels for 6% -> 5%
where the time goes in v1:
time: 328 us
  waiting for transfers between devices  133 us (41%)
  blocking collectives  100 us (30%)
  Pallas kernels  44.4 us (14%)
  starting transfers between devices  30.9 us (9%)
  other arithmetic  8.71 us (3%)
  local copies, waits for them, and re-layouts  7.13 us (2%)
    ppermute x6, waiting for transfers between devices, chip_swap(): return lax.ppermute(x, 'feat', [(0, 2), (2, 0), (1, 3), (3, 1)])  115 us
    all_to_all x1, blocking collectives, exchange(): return lax.all_to_all(x, 'rows', split_axis=0, concat_axis=0, tiled=True)  100 us
    all_to_all x2, starting transfers between devices, exchange(): return lax.all_to_all(x, 'rows', split_axis=0, concat_axis=0, tiled=True)  18.2 us
    all_to_all x2, waiting for transfers between devices, exchange(): return lax.all_to_all(x, 'rows', split_axis=0, concat_axis=0, tiled=True)  13.4 us
    pallas_call x1, Pallas kernels, aggregate(): pl.pallas_call(functools.partial(aggregate_kernel, lists, slots), grid_sp...  11.8 us
    pallas_call x1, Pallas kernels, terms(): pl.pallas_call(functools.partial(terms_kernel, lists, slots, main // 2),...  11.4 us
    pallas_call x1, Pallas kernels, middle(): pl.pallas_call(functools.partial(middle_kernel, step), grid=(blocks // st...  8.18 us
    ppermute x6, starting transfers between devices, chip_swap(): return lax.ppermute(x, 'feat', [(0, 2), (2, 0), (1, 3), (3, 1)])  7.29 us
  transfers between devices with their start and end apart: 22, of which 7 were waited for; matrix products, arithmetic and copies ran while one was open for 2% of the time, Pallas kernels for 5%

profile of v1, /device:TPU:0, one launch (start us, length us, event | category | flops | bytes accessed | tf_op | source)
XLA Modules:
  0.0 327.9 jit_solution(10969981315986340316)
XLA Ops:
  1.3 0.7 compare_select_fusion
  2.0 2.1 collective-permute-start.1
  4.1 0.2 collective-permute-start.5
  4.3 0.3 collective-permute-start.4
  4.6 1.4 slice_bitcast_fusion
  6.0 1.8 collective-permute-start.3
  8.1 1.1 collective-permute-done.2
  9.3 0.3 fusion.15
  9.7 0.6 reduce_max.18
  10.3 1.3 concatenate.48
  11.5 10.3 %all-to-all-start.2 = ((s32[32,1,128]{2,1,0:T(1,128)}), s32[32,1,128]{2,1,0:T(1,128)S(1)}, u32[]{:S(2)}, u32[]{:S(2)}) async-start(s32[32,1,128]{2,1,0:T(1,128)} %bitcast.8), calls=%async_computation.2 | async-start | bytes 32768 | tf_op jit(solution)/shard_map/all_to_all | solution.py:491
  21.9 0.3 fusion
  22.4 0.6 add_select_fusion.place
  23.0 0.7 pad_add_fusion.2.target
  23.7 0.6 convert_element_type.43.again
  24.3 0.6 reduce_sum.47.live
  25.0 1.2 collective-permute-done.6
  26.3 0.8 pad_maximum_fusion.weight
  27.1 13.4 %all-to-all-done.2 = s32[32,1,128]{2,1,0:T(1,128)S(1)} async-done(((s32[32,1,128]{2,1,0:T(1,128)}), s32[32,1,128]{2,1,0:T(1,128)S(1)}, u32[]{:S(2)}, u32[]{:S(2)}) %all-to-all-start.2) | async-done | bytes 16416 | tf_op jit(solution)/shard_map/all_to_all | solution.py:491
  40.7 0.8 slice_reduce_fusion.1.count
  41.5 0.7 slice_reduce_fusion
  42.2 0.6 select_reduce_fusion
  42.8 0.6 broadcast_add_fusion.index
  44.1 5.3 %shard_map.103 = (bf16[32,896,128]{2,1,0:T(8,128)(2,1)}, bf16[32,128,128]{2,1,0:T(8,128)(2,1)S(1)}) custom-call(s32[32,16]{1,0:T(8,128)} %broadcast_add_fusion.index, s32[32]{0:T(128)} %slice_reduce_fusion.1.count, bf16[64,6144]{1,0:T(8,128)(2,1)} %features.1), custom_call_target="tpu_custom_call" | custom-call | bytes 8388608 | tf_op jit(solution)/shard_map/pallas_call | solution.py:103
  49.4 1.0 copy-done.4
  50.3 7.9 %all-to-all-start.3 = ((bf16[32,896,128]{2,1,0:T(8,128)(2,1)}), bf16[32,896,128]{2,1,0:T(8,128)(2,1)}, u32[]{:S(2)}, u32[]{:S(2)}) async-start(bf16[32,896,128]{2,1,0:T(8,128)(2,1)} %get-tuple-element.40), calls=%async_computation.3 | async-start | bytes 14680064 | tf_op jit(solution)/shard_map/all_to_all | solution.py:491
  58.4 1.1 collective-permute-start.8
  59.5 0.2 collective-permute-start.9
  59.7 95.3 %collective-permute-done.8.refs_3_ = bf16[24,128,128]{2,1,0:T(8,128)(2,1)S(1)} collective-permute-done((bf16[24,128,128]{2,1,0:T(8,128)(2,1)S(1)}, bf16[24,128,128]{2,1,0:T(8,128)(2,1)S(1)}, u32[]{:S(2)}, u32[]{:S(2)}) %collective-permute-start.8) | collective-permute-done | bytes 786464 | tf_op jit(solution)/shard_map/ppermute | solution.py:31
  155.0 1.0 collective-permute-start.15
  156.0 1.3 copy-done.1
  157.3 1.1 copy-done.3
  158.4 11.8 %shard_map.104.a0 = bf16[48,64,128]{2,1,0:T(8,128)(2,1)} custom-call(s32[256]{0:T(256)} %add_select_fusion.place, s32[256]{0:T(256)} %pad_add_fusion.2.target, s32[4]{0:T(128)} %reduce_sum.47.live, s32[32]{0:T(128)} %copy-done.14, bf16[32,14,64,128]{3,2,1,0:T(8,128)(2,1)} %bitcast.15.panels, bf16[32,2,64,128]{3,2,1,0:T(8,128)(2,1)} %bitcast.43, ...), custom_call_target="tpu_custom_call" | custom-call | flops 536870912 | bytes 15728640 | tf_op jit(solution)/shard_map/pallas_call | solution.py:213
  170.2 1.1 collective-permute-start.12
  171.3 4.3 %collective-permute-done.15.c2 = bf16[64,6144]{1,0:T(8,128)(2,1)} collective-permute-done((bf16[64,6144]{1,0:T(8,128)(2,1)}, bf16[64,6144]{1,0:T(8,128)(2,1)}, u32[]{:S(2)}, u32[]{:S(2)}) %collective-permute-start.15) | collective-permute-done | bytes 786464 | tf_op jit(solution)/shard_map/ppermute | solution.py:31
  175.7 0.5 collective-permute-start.11
  176.2 15.9 %collective-permute-done.12.a2 = bf16[48,64,128]{2,1,0:T(8,128)(2,1)S(1)} collective-permute-done((bf16[48,64,128]{2,1,0:T(8,128)(2,1)}, bf16[48,64,128]{2,1,0:T(8,128)(2,1)S(1)}, u32[]{:S(2)}, u32[]{:S(2)}) %collective-permute-start.12) | collective-permute-done | bytes 786464 | tf_op jit(solution)/shard_map/ppermute | solution.py:31
  192.1 2.2 collective-permute-done.13.a3
  194.4 0.9 copy-done.11
  195.2 8.2 %shard_map.105 = (bf16[64,6144]{1,0:T(8,128)(2,1)}, bf16[48,64,128]{2,1,0:T(8,128)(2,1)}, bf16[128,128]{1,0:T(8,128)(2,1)}) custom-call(bf16[256,256]{1,0:T(8,128)(2,1)} %pad_maximum_fusion.weight, bf16[48,64,128]{2,1,0:T(8,128)(2,1)} %shard_map.104.a0, bf16[48,64,128]{2,1,0:T(8,128)(2,1)} %copy-done.10, bf16[48,64,128]{2,1,0:T(8,128)(2,1)} %copy-done.7, ...), custom_call_target="tpu_custom_call" | custom-call | flops 1207959552 | bytes 7864320 | tf_op jit(solution)/shard_map/pallas_call | solution.py:281
  203.4 11.4 %shard_map.106 = (bf16[32,928,128]{2,1,0:T(8,128)(2,1)}, bf16[32,128,128]{2,1,0:T(8,128)(2,1)S(1)}) custom-call(s32[256]{0:T(256)} %add_select_fusion.place, s32[256]{0:T(256)} %pad_add_fusion.2.target, s32[256]{0:T(256)} %convert_element_type.43.again, s32[4]{0:T(128)} %reduce_sum.47.live, s32[32]{0:T(128)} %copy-done.14, ...), custom_call_target="tpu_custom_call" | custom-call | flops 536870912 | bytes 15728640 | tf_op jit(solution)/shard_map/pallas_call | solution.py:384
  214.8 100.3 %all_to_all.32.incoming = bf16[32,928,128]{2,1,0:T(8,128)(2,1)} all-to-all(bf16[32,928,128]{2,1,0:T(8,128)(2,1)} %get-tuple-element.51), channel_id=1, replica_groups=mesh['rows'=32,'feat'=4] {'rows'}, dimensions={0} | all-to-all | bytes 15204352 | tf_op jit(solution)/shard_map/all_to_all | solution.py:491
  315.1 1.6 shard_map.108
  316.7 0.4 collective-permute-start.17
  317.1 1.3 collective-permute-start.18
  318.4 2.4 collective-permute-start.19
  320.8 6.2 %shard_map.107 = bf16[64,6144]{1,0:T(8,128)(2,1)} custom-call(s32[32,16]{1,0:T(8,128)} %broadcast_add_fusion.index, s32[32]{0:T(128)} %slice_reduce_fusion.1.count, bf16[32,928,128]{2,1,0:T(8,128)(2,1)} %all_to_all.32.incoming, bf16[32,128,128]{2,1,0:T(8,128)(2,1)S(1)} %get-tuple-element.82.over), custom_call_target="tpu_custom_call" | custom-call | flops 3670016 | bytes 7340032 | tf_op jit(solution)/shard_map/pallas_call | solution.py:467
  327.2 0.7 maximum_multiply_fusion
  (80 shorter events, 1.2 us)
Async XLA Ops:
  0.6 7.3 %copy-start.17 = (s32[1,64]{1,0:T(1,128)S(1)}, s32[1,64]{1,0:T(1,128)}, u32[]{:S(2)}) copy-start(s32[1,64]{1,0:T(1,128)} %param.16) | copy-start | bytes 772
  0.6 7.2 %copy-start.16 = (s32[1,64,1]{1,2,0:T(1,128)S(1)}, s32[1,64,1]{1,2,0:T(1,128)}, u32[]{:S(2)}) copy-start(s32[1,64,1]{1,2,0:T(1,128)} %param.17) | copy-start | bytes 772
  0.7 7.2 %copy-start.15 = (s32[1,64]{1,0:T(1,128)S(1)}, s32[1,64]{1,0:T(1,128)}, u32[]{:S(2)}) copy-start(s32[1,64]{1,0:T(1,128)} %param.18) | copy-start | bytes 772
  0.7 7.2 %copy-start.13 = (bf16[64,256]{1,0:T(8,128)(2,1)S(1)}, bf16[64,256]{1,0:T(8,128)(2,1)}, u32[]{:S(2)}) copy-start(bf16[64,256]{1,0:T(8,128)(2,1)} %param.13) | copy-start | bytes 98308
  2.0 5.9 %collective-permute-start.1 = (s32[2,64]{1,0:T(2,128)S(1)}, s32[2,64]{1,0:T(2,128)S(1)}, u32[]{:S(2)}, u32[]{:S(2)}) collective-permute-start(s32[2,64]{1,0:T(2,128)S(1)} %pad_add_fusion), channel_id=1, source_target_pairs={{0,2},{2,0},{1,3},{3,1},{4,6},{6,4},{5,7},{7,5},{8,10},{10,8},{9,1... | collective-permute-start | bytes 1544 | tf_op jit(solution)/shard_map/ppermute | solution.py:31
  4.1 3.9 %collective-permute-start = (s32[2,64]{1,0:T(2,128)S(1)}, s32[2,64]{1,0:T(2,128)S(1)}, u32[]{:S(2)}, u32[]{:S(2)}) collective-permute-start(s32[2,64]{1,0:T(2,128)S(1)} %pad_add_fusion), channel_id=1, source_target_pairs={{0,1},{1,0},{2,3},{3,2},{4,5},{5,4},{6,7},{7,6},{8,9},{9,8},{10,11... | collective-permute-start | bytes 1544 | tf_op jit(solution)/shard_map/ppermute | solution.py:27
  4.1 20.9 %collective-permute-start.5 = (bf16[64,256]{1,0:T(8,128)(2,1)}, bf16[64,256]{1,0:T(8,128)(2,1)S(1)}, u32[]{:S(2)}, u32[]{:S(2)}) collective-permute-start(bf16[64,256]{1,0:T(8,128)(2,1)} %param.13), channel_id=1, source_target_pairs={{0,2},{2,0},{1,3},{3,1},{4,6},{6,4},{5,7},{7,5},{8,10},{10,8},{9,1... | collective-permute-start | bytes 98312 | tf_op jit(solution)/shard_map/ppermute | solution.py:31
  4.3 20.7 %collective-permute-start.4 = (bf16[64,256]{1,0:T(8,128)(2,1)}, bf16[64,256]{1,0:T(8,128)(2,1)S(1)}, u32[]{:S(2)}, u32[]{:S(2)}) collective-permute-start(bf16[64,256]{1,0:T(8,128)(2,1)} %param.13), channel_id=1, source_target_pairs={{0,1},{1,0},{2,3},{3,2},{4,5},{5,4},{6,7},{7,6},{8,9},{9,8},{10,11... | collective-permute-start | bytes 98312 | tf_op jit(solution)/shard_map/ppermute | solution.py:27
  6.0 34.5 %collective-permute-start.3 = (bf16[40,128,128]{2,1,0:T(8,128)(2,1)S(1)}, bf16[40,128,128]{2,1,0:T(8,128)(2,1)S(1)}, u32[]{:S(2)}, u32[]{:S(2)}) collective-permute-start(bf16[40,128,128]{2,1,0:T(8,128)(2,1)S(1)} %slice_bitcast_fusion), channel_id=1, source_target_pairs={{0,2},{2,0},{1,3},{3,1},{4,6},{6,4},{5,7},{7,5},{8,10},{10,8},{9,1... | collective-permute-start | bytes 3932168 | tf_op jit(solution)/shard_map/ppermute | solution.py:31
  8.0 1.2 collective-permute-start.2
  9.6 39.7 %copy-start.14 = (s32[32]{0:T(128)}, s32[32]{0:T(128)S(1)}, u32[]{:S(2)}) copy-start(s32[32]{0:T(128)S(1)} %convert_reduce_fusion.used) | copy-start | bytes 388
  11.5 29.0 %all-to-all-start.2 = ((s32[32,1,128]{2,1,0:T(1,128)}), s32[32,1,128]{2,1,0:T(1,128)S(1)}, u32[]{:S(2)}, u32[]{:S(2)}) async-start(s32[32,1,128]{2,1,0:T(1,128)} %bitcast.8), calls=%async_computation.2 | async-start | bytes 32768 | tf_op jit(solution)/shard_map/all_to_all | solution.py:491
  25.0 1.2 collective-permute-start.6
  40.5 19.0 %copy-start.2 = (bf16[40,128,128]{2,1,0:T(8,128)(2,1)}, bf16[40,128,128]{2,1,0:T(8,128)(2,1)S(1)}, u32[]{:S(2)}) copy-start(bf16[40,128,128]{2,1,0:T(8,128)(2,1)S(1)} %collective-permute-done.3.refs_2_) | copy-start | bytes 3932164
  49.4 1.0 copy-start.4
  50.3 7.9 %copy-start = (bf16[1,64,128,128]{3,2,1,0:T(8,128)(2,1)S(1)}, bf16[1,64,128,128]{3,2,1,0:T(8,128)(2,1)}, u32[]{:S(2)}) copy-start(bf16[1,64,128,128]{3,2,1,0:T(8,128)(2,1)} %param.15) | copy-start | bytes 6291460
  50.3 108.1 %all-to-all-start.3 = ((bf16[32,896,128]{2,1,0:T(8,128)(2,1)}), bf16[32,896,128]{2,1,0:T(8,128)(2,1)}, u32[]{:S(2)}, u32[]{:S(2)}) async-start(bf16[32,896,128]{2,1,0:T(8,128)(2,1)} %get-tuple-element.40), calls=%async_computation.3 | async-start | bytes 14680064 | tf_op jit(solution)/shard_map/all_to_all | solution.py:491
  58.3 97.8 %collective-permute-start.7 = (bf16[64,128,128]{2,1,0:T(8,128)(2,1)S(1)}, bf16[64,128,128]{2,1,0:T(8,128)(2,1)S(1)}, u32[]{:S(2)}, u32[]{:S(2)}) collective-permute-start(bf16[64,128,128]{2,1,0:T(8,128)(2,1)S(1)} %bitcast.42), channel_id=1, source_target_pairs={{0,1},{1,0},{2,3},{3,2},{4,5},{5,4},{6,7},{7,6},{8,9},{9,8},{10,11... | collective-permute-start | bytes 6291464 | tf_op jit(solution)/shard_map/ppermute | solution.py:27
  58.4 96.6 %collective-permute-start.8 = (bf16[24,128,128]{2,1,0:T(8,128)(2,1)S(1)}, bf16[24,128,128]{2,1,0:T(8,128)(2,1)S(1)}, u32[]{:S(2)}, u32[]{:S(2)}) collective-permute-start(bf16[24,128,128]{2,1,0:T(8,128)(2,1)S(1)} %slice_bitcast_fusion.1), channel_id=1, source_target_pairs={{0,2},{2,0},{1,3},{3,1},{4,6},{6,4},{5,7},{7,5},{8,10},{10,8},{9,1... | collective-permute-start | bytes 2359304 | tf_op jit(solution)/shard_map/ppermute | solution.py:31
  59.5 97.8 %collective-permute-start.9 = (bf16[40,128,128]{2,1,0:T(8,128)(2,1)S(1)}, bf16[40,128,128]{2,1,0:T(8,128)(2,1)S(1)}, u32[]{:S(2)}, u32[]{:S(2)}) collective-permute-start(bf16[40,128,128]{2,1,0:T(8,128)(2,1)S(1)} %collective-permute-done.3.refs_2_), channel_id=1, source_target_pairs={{0,1},{1,0},{2,3},{3,2},{4,5},{5,4},{6,7},{7,6},{8,9},{9,8},{10,11... | collective-permute-start | bytes 3932168 | tf_op jit(solution)/shard_map/ppermute | solution.py:27
  155.0 2.3 copy-start.5
  155.0 3.4 %collective-permute-start.10 = (bf16[24,128,128]{2,1,0:T(8,128)(2,1)S(1)}, bf16[24,128,128]{2,1,0:T(8,128)(2,1)}, u32[]{:S(2)}, u32[]{:S(2)}) collective-permute-start(bf16[24,128,128]{2,1,0:T(8,128)(2,1)S(1)} %collective-permute-done.8.refs_3_), channel_id=1, source_target_pairs={{0,1},{1,0},{2,3},{3,2},{4,5},{5,4},{6,7},{7,6},{8,9},{9,8},{10,11... | collective-permute-start | bytes 2359304 | tf_op jit(solution)/shard_map/ppermute | solution.py:27
  155.0 20.7 %collective-permute-start.15 = (bf16[64,6144]{1,0:T(8,128)(2,1)}, bf16[64,6144]{1,0:T(8,128)(2,1)}, u32[]{:S(2)}, u32[]{:S(2)}) collective-permute-start(bf16[64,6144]{1,0:T(8,128)(2,1)} %c0), channel_id=1, source_target_pairs={{0,2},{2,0},{1,3},{3,1},{4,6},{6,4},{5,7},{7,5},{8,10},{10,8},{9,1... | collective-permute-start | bytes 2359304 | tf_op jit(solution)/shard_map/ppermute | solution.py:31
  156.0 1.3 copy-start.1
  157.3 1.1 copy-start.3
  158.4 12.9 %copy-start.6 = (bf16[64,6144]{1,0:T(8,128)(2,1)S(1)}, bf16[64,6144]{1,0:T(8,128)(2,1)}, u32[]{:S(2)}) copy-start(bf16[64,6144]{1,0:T(8,128)(2,1)} %c0) | copy-start | bytes 2359300
  170.2 21.8 %collective-permute-start.12 = (bf16[48,64,128]{2,1,0:T(8,128)(2,1)}, bf16[48,64,128]{2,1,0:T(8,128)(2,1)S(1)}, u32[]{:S(2)}, u32[]{:S(2)}) collective-permute-start(bf16[48,64,128]{2,1,0:T(8,128)(2,1)} %shard_map.104.a0), channel_id=1, source_target_pairs={{0,2},{2,0},{1,3},{3,1},{4,6},{6,4},{5,7},{7,5},{8,10},{10,8},{9,1... | collective-permute-start | bytes 2359304 | tf_op jit(solution)/shard_map/ppermute | solution.py:31
  171.3 20.7 %collective-permute-start.14 = (bf16[64,6144]{1,0:T(8,128)(2,1)S(1)}, bf16[64,6144]{1,0:T(8,128)(2,1)S(1)}, u32[]{:S(2)}, u32[]{:S(2)}) collective-permute-start(bf16[64,6144]{1,0:T(8,128)(2,1)S(1)} %copy-done.6), channel_id=1, source_target_pairs={{0,1},{1,0},{2,3},{3,2},{4,5},{5,4},{6,7},{7,6},{8,9},{9,8},{10,11... | collective-permute-start | bytes 2359304 | tf_op jit(solution)/shard_map/ppermute | solution.py:27
  175.7 16.4 %collective-permute-start.16 = (bf16[64,6144]{1,0:T(8,128)(2,1)}, bf16[64,6144]{1,0:T(8,128)(2,1)S(1)}, u32[]{:S(2)}, u32[]{:S(2)}) collective-permute-start(bf16[64,6144]{1,0:T(8,128)(2,1)} %collective-permute-done.15.c2), channel_id=1, source_target_pairs={{0,1},{1,0},{2,3},{3,2},{4,5},{5,4},{6,7},{7,6},{8,9},{9,8},{10,11... | collective-permute-start | bytes 2359304 | tf_op jit(solution)/shard_map/ppermute | solution.py:27
  175.7 16.4 %collective-permute-start.11 = (bf16[48,64,128]{2,1,0:T(8,128)(2,1)}, bf16[48,64,128]{2,1,0:T(8,128)(2,1)S(1)}, u32[]{:S(2)}, u32[]{:S(2)}) collective-permute-start(bf16[48,64,128]{2,1,0:T(8,128)(2,1)} %shard_map.104.a0), channel_id=1, source_target_pairs={{0,1},{1,0},{2,3},{3,2},{4,5},{5,4},{6,7},{7,6},{8,9},{9,8},{10,11... | collective-permute-start | bytes 2359304 | tf_op jit(solution)/shard_map/ppermute | solution.py:27
  192.0 2.3 copy-start.7
  192.0 2.3 collective-permute-start.13
  192.0 2.3 copy-start.8
  192.1 2.3 copy-start.9
  192.1 2.2 copy-start.10
  194.3 0.9 copy-start.11
  316.7 10.3 %collective-permute-start.17 = (f32[32,128]{1,0:T(8,128)}, f32[32,128]{1,0:T(8,128)S(1)}, u32[]{:S(2)}, u32[]{:S(2)}) collective-permute-start(f32[32,128]{1,0:T(8,128)} %shard_map.108), channel_id=1, source_target_pairs={{0,4},{4,0},{8,12},{12,8},{16,20},{20,16},{24,28},{28,24},{32,36},... | collective-permute-start | bytes 49160 | tf_op jit(solution)/shard_map/ppermute | solution.py:522
  317.1 9.9 %collective-permute-start.18 = (f32[32,128]{1,0:T(8,128)}, f32[32,128]{1,0:T(8,128)S(1)}, u32[]{:S(2)}, u32[]{:S(2)}) collective-permute-start(f32[32,128]{1,0:T(8,128)} %shard_map.108), channel_id=1, source_target_pairs={{0,12},{4,8},{8,4},{12,0},{16,28},{20,24},{24,20},{28,16},{32,44},... | collective-permute-start | bytes 49160 | tf_op jit(solution)/shard_map/ppermute | solution.py:522
  318.4 8.6 %collective-permute-start.19 = (f32[32,128]{1,0:T(8,128)}, f32[32,128]{1,0:T(8,128)S(1)}, u32[]{:S(2)}, u32[]{:S(2)}) collective-permute-start(f32[32,128]{1,0:T(8,128)} %shard_map.108), channel_id=1, source_target_pairs={{0,8},{4,12},{8,0},{12,4},{16,24},{20,28},{24,16},{28,20},{32,40},... | collective-permute-start | bytes 49160 | tf_op jit(solution)/shard_map/ppermute | solution.py:522
  320.8 6.2 %copy-start.12 = (f32[32,128]{1,0:T(8,128)S(1)}, f32[32,128]{1,0:T(8,128)}, u32[]{:S(2)}) copy-start(f32[32,128]{1,0:T(8,128)} %shard_map.108) | copy-start | bytes 49156
